TPU v7x, 256 devices: a whole 4x4x8 slice. The times are simulated.
256 devices in a mesh: tile: 32 (over y, x, core), pair: 8 (over z).
Axes of the slice: x: 4, y: 4, z: 8, core: 2. Of those that a mesh axis runs over, the one named last changes fastest.
Arguments:
- l_tiles: bfloat16 [768, 32768], P('pair', 'tile'), may hold values from -6 to 6
- nz_lists: int32 [8, 32, 8], P('pair', 'tile'), may hold values from 0 to 9, as said below
- v_slab: bfloat16 [32, 8, 1280, 1280], P('tile', 'pair'), may hold values from -0.046875 to 0.046875
Outputs:
- ladder: float32 [768, 40960], P('pair', 'tile')
Inputs may be any that keep to these rules, and one draw needn't show every extreme that they name: Each row nz_lists(b, g, :) names 8 different blocks of the 10 in group g, in increasing order.
All inputs are finite; a program needn't handle non-finite values.
Results may differ from a plain program's by a relative error of at most 0.0003.
Values may be sent and summed in bfloat16 or wider, within the bound.
A program may use at most 64 MiB of HBM per device.

v0:
```python
import jax
import jax.numpy as jnp
from jax import lax
from jax.sharding import PartitionSpec as P

KB = 10


def from_behind(value, axis, steps):
    count = lax.axis_size(axis)
    pairs = [(source, (source + steps) % count) for source in range(count)]
    return lax.ppermute(value, axis, pairs)


def expand_rows(tile_rows, list_rows):
    batches = list_rows.shape[0]
    entries = list_rows.shape[-1]
    tile_size = tile_rows.shape[1] // entries
    per_batch = tile_rows.shape[0] // batches
    shaped = tile_rows.reshape(batches, per_batch, entries, tile_size)
    flat_lists = list_rows.reshape(batches, entries)
    onehot = (flat_lists[:, :, None] == jnp.arange(KB, dtype=jnp.int32)[None, None, :]).astype(
        jnp.bfloat16
    )
    dense_rows = jnp.einsum("bpeu,bek->bpku", shaped, onehot, preferred_element_type=jnp.float32)
    return dense_rows.astype(jnp.bfloat16).reshape(batches * per_batch, KB * tile_size)


def shards(l_tiles, nz_lists, v_slab):
    pair_count = lax.axis_size("pair")
    pair_index = lax.axis_index("pair")
    hop_count = pair_count.bit_length() - 1
    own_tiles, own_lists = (
        lax.all_gather(l_tiles, "pair", axis=0, tiled=True),
        lax.all_gather(nz_lists, "pair", axis=0, tiled=True),
    )
    far_tiles, far_lists = (own_tiles, own_lists)
    for bit_pos in range(hop_count):
        arrived_tiles, arrived_lists = from_behind((far_tiles, far_lists), "tile", -(1 << bit_pos))
        chosen = pair_index >> bit_pos & 1 == 1
        far_tiles = jnp.where(chosen, arrived_tiles, far_tiles)
        far_lists = jnp.where(chosen, arrived_lists, far_lists)
    dense_own = expand_rows(own_tiles, own_lists)
    dense_far = expand_rows(far_tiles, far_lists)
    v_block = v_slab[0, 0]
    block_width = v_block.shape[0]
    row_ids = lax.broadcasted_iota(jnp.int32, (block_width, block_width), 0)
    col_ids = lax.broadcasted_iota(jnp.int32, (block_width, block_width), 1)
    offdiag = pair_index > 0
    direct_block = jnp.where(offdiag | (row_ids <= col_ids), v_block, jnp.zeros_like(v_block))
    mirror_block = jnp.where(offdiag | (row_ids < col_ids), v_block, jnp.zeros_like(v_block))
    direct = jnp.dot(dense_own, direct_block, preferred_element_type=jnp.float32)
    mirror = lax.dot_general(
        dense_far, mirror_block, (((1,), (1,)), ((), ())), preferred_element_type=jnp.float32
    )
    carried = direct
    for bit_pos in range(hop_count):
        arrived = from_behind(carried, "tile", 1 << bit_pos)
        chosen = pair_index >> bit_pos & 1 == 1
        carried = jnp.where(chosen, arrived, carried)
    ladder = lax.psum_scatter(carried + mirror, "pair", scatter_dimension=0, tiled=True)
    return ladder


def solution(mesh):
    placed = (P("pair", "tile"), P("pair", "tile", None), P("tile", "pair", None, None))
    return jax.shard_map(
        shards, mesh=mesh, in_specs=placed, out_specs=P("pair", "tile"), check_vma=False
    )
```

profile of v0, /device:TPU:32, one launch (start us, length us, event | category | flops | bytes accessed | tf_op | source)
XLA Modules:
  0.0 396.3 jit_solution(405084138202171451)
XLA Ops:
  6.5 0.0 all-gather.2.cloned.1.call-start
  6.5 0.7 all-gather.2.cloned.1.call-update
  7.3 0.0 reduce-scatter.2.cloned.1.call-start
  7.3 17.1 %all_gather.6 = s32[8,1,8]{2,1,0:T(1,128)S(1)} all-gather(s32[1,1,8]{2,1,0:T(1,128)} %param.4), channel_id=1, replica_groups=mesh['tile'=32,'pair'=8] {'pair'}, dimensions={0}, use_global_device_ids=true | all-gather | bytes 288 | tf_op jit(solution)/shard_map/all_gather | solution.py:35
  24.4 27.1 %all-gather.2.cloned.1.call-done = bf16[768,1024]{1,0:T(8,128)(2,1)} async-done(((bf16[96,1024]{1,0:T(8,128)(2,1)}), bf16[768,1024]{1,0:T(8,128)(2,1)}) %all-gather.2.cloned.1.call-update) | async-done | bytes 1572880 | tf_op jit(solution)/shard_map/all_gather | solution.py:34
  51.5 0.0 copy-start.1
  51.5 2.0 copy.16
  53.5 1.1 convolution_convert_fusion.1
  54.6 0.0 copy-done.1
  54.6 4.6 %fusion.8 = f32[768,1280]{1,0:T(8,128)} fusion(bf16[1,1,1280,1280]{3,2,1,0:T(8,128)(2,1)S(1)} %copy-done.1, pred[]{:T(512)S(6)} %gt.3, bf16[96,8,10,128]{3,2,1,0:T(8,128)(2,1)S(1)} %bitcast.52), kind=kOutput, calls=%fused_computation.10 | convolution fusion | flops 2521497600 | bytes 9175041 | tf_op jit(solution)/shard_map/dot_general | solution.py:52
  59.2 0.0 collective-permute-start
  59.2 0.0 copy-start
  59.2 48.8 %collective-permute-done = f32[768,1280]{1,0:T(8,128)} collective-permute-done((f32[768,1280]{1,0:T(8,128)}, f32[768,1280]{1,0:T(8,128)}, u32[]{:S(2)}, u32[]{:S(2)}) %collective-permute-start) | collective-permute-done | bytes 3932192 | tf_op jit(solution)/shard_map/ppermute | solution.py:12
  107.9 4.5 %broadcast_select_fusion = f32[768,1280]{1,0:T(8,128)} fusion(f32[768,1280]{1,0:T(8,128)} %collective-permute-done, f32[768,1280]{1,0:T(8,128)} %fusion.8, pred[]{:T(512)S(6)} %eq.44), kind=kLoop, calls=%fused_computation.19 | loop fusion | flops 983040 | bytes 11796481 | tf_op jit(solution)/shard_map/jit(_where)/select_n | solution.py:60
  112.4 0.0 collective-permute-start.1
  112.4 0.0 copy-done
  112.4 0.5 collective-permute-start.6
  112.9 17.9 %collective-permute-done.6 = bf16[768,1024]{1,0:T(8,128)(2,1)S(1)} collective-permute-done((bf16[768,1024]{1,0:T(8,128)(2,1)S(1)}, bf16[768,1024]{1,0:T(8,128)(2,1)S(1)}, u32[]{:S(2)}, u32[]{:S(2)}) %collective-permute-start.6) | collective-permute-done | bytes 1572896 | tf_op jit(solution)/shard_map/ppermute | solution.py:12
  130.8 0.2 broadcast_select_fusion.2
  131.0 5.0 %collective-permute-start.7 = (bf16[768,1024]{1,0:T(8,128)(2,1)S(1)}, bf16[768,1024]{1,0:T(8,128)(2,1)}, u32[]{:S(2)}, u32[]{:S(2)}) collective-permute-start(bf16[768,1024]{1,0:T(8,128)(2,1)S(1)} %broadcast_select_fusion.2), channel_id=1, source_target_pairs={{0,240},{8,248},{16,0},{24,8},{32,16},{40,24},{48,32},{56,40},{64,... | collective-permute-start | bytes 4718600 | tf_op jit(solution)/shard_map/ppermute | solution.py:12
  135.9 62.8 %collective-permute-done.1 = f32[768,1280]{1,0:T(8,128)} collective-permute-done((f32[768,1280]{1,0:T(8,128)}, f32[768,1280]{1,0:T(8,128)}, u32[]{:S(2)}, u32[]{:S(2)}) %collective-permute-start.1) | collective-permute-done | bytes 3932192 | tf_op jit(solution)/shard_map/ppermute | solution.py:12
  198.7 4.5 %broadcast_select_fusion.1 = f32[768,1280]{1,0:T(8,128)} fusion(f32[768,1280]{1,0:T(8,128)} %collective-permute-done.1, f32[768,1280]{1,0:T(8,128)} %broadcast_select_fusion, pred[]{:T(512)S(6)} %eq.43), kind=kLoop, calls=%fused_computation.20 | loop fusion | flops 983040 | bytes 11796481 | tf_op jit(solution)/shard_map/jit(_where)/select_n | solution.py:60
  203.1 0.0 collective-permute-start.2
  203.1 0.0 collective-permute-done.7
  203.2 0.2 broadcast_select_fusion.3
  203.3 5.7 %collective-permute-start.8 = (bf16[768,1024]{1,0:T(8,128)(2,1)S(1)}, bf16[768,1024]{1,0:T(8,128)(2,1)S(1)}, u32[]{:S(2)}, u32[]{:S(2)}) collective-permute-start(bf16[768,1024]{1,0:T(8,128)(2,1)S(1)} %broadcast_select_fusion.3), channel_id=1, source_target_pairs={{0,224},{8,232},{16,240},{24,248},{32,0},{40,8},{48,16},{56,24},{6... | collective-permute-start | bytes 4718600 | tf_op jit(solution)/shard_map/ppermute | solution.py:12
  209.0 0.0 collective-permute-start.3
  209.0 1.3 collective-permute-done.3
  210.4 110.6 %collective-permute-start.4 = (s32[8,1,8]{2,0,1:T(8,128)S(1)}, s32[8,1,8]{2,0,1:T(8,128)S(1)}, u32[]{:S(2)}, u32[]{:S(2)}) collective-permute-start(s32[8,1,8]{2,0,1:T(8,128)S(1)} %broadcast_select_fusion.4), channel_id=1, source_target_pairs={{0,240},{8,248},{16,0},{24,8},{32,16},{40,24},{48,32},{56,40},{64,... | collective-permute-start | bytes 776 | tf_op jit(solution)/shard_map/ppermute | solution.py:12
  321.0 1.3 collective-permute-done.4
  322.4 1.7 collective-permute-start.5
  324.1 3.4 collective-permute-done.5
  327.5 0.0 collective-permute-done.8
  327.5 0.2 select_bitcast_fusion
  327.6 0.0 copy-start.2
  327.7 0.4 copy.18
  328.1 1.1 convolution_convert_fusion
  329.2 0.4 copy-done.2
  329.6 2.7 fusion.5
  332.3 0.0 collective-permute-done.2
  332.3 4.7 %select_add_fusion = f32[768,1280]{1,0:T(8,128)} fusion(f32[768,1280]{1,0:T(8,128)S(1)} %fusion.5, f32[768,1280]{1,0:T(8,128)} %collective-permute-done.2, f32[768,1280]{1,0:T(8,128)} %broadcast_select_fusion.1, pred[]{:T(512)S(6)} %eq.42), kind=kLoop, calls=%fused_computation.6 | loop fusion | flops 1966080 | bytes 15728641 | tf_op jit(solution)/shard_map/add | solution.py:61
  337.1 0.0 reduce-scatter.2.cloned.1.call-update
  337.1 52.4 %reduce-scatter.2.cloned.1.call-done = f32[96,1280]{1,0:T(8,128)} async-done(((f32[768,1280]{1,0:T(8,128)}), f32[96,1280]{1,0:T(8,128)}) %reduce-scatter.2.cloned.1.call-update) | async-done | bytes 491536 | tf_op jit(solution)/shard_map/reduce_scatter | solution.py:61
  (3 shorter events, 0.0 us)
Async XLA Ops:
  6.5 44.9 %all-gather.2.cloned.1.call-start = ((), (), s32[]{:S(2)}) async-start(), calls=%async_computation.1 | async-start | bytes 1769472 | tf_op jit(solution)/shard_map/all_gather | solution.py:34
  7.3 382.2 %reduce-scatter.2.cloned.1.call-start = ((), (), s32[]{:S(2)}) async-start(), calls=%async_computation.2 | async-start | bytes 4423680 | tf_op jit(solution)/shard_map/reduce_scatter | solution.py:61
  51.5 3.1 copy-start.1
  59.2 48.8 %collective-permute-start = (f32[768,1280]{1,0:T(8,128)}, f32[768,1280]{1,0:T(8,128)}, u32[]{:S(2)}, u32[]{:S(2)}) collective-permute-start(f32[768,1280]{1,0:T(8,128)} %fusion.8), channel_id=1, source_target_pairs={{0,8},{8,16},{16,24},{24,32},{32,40},{40,48},{48,56},{56,64},{64,7... | collective-permute-start | bytes 11796488 | tf_op jit(solution)/shard_map/ppermute | solution.py:12
  59.2 53.2 %copy-start = (bf16[768,1024]{1,0:T(8,128)(2,1)S(1)}, bf16[768,1024]{1,0:T(8,128)(2,1)}, u32[]{:S(2)}) copy-start(bf16[768,1024]{1,0:T(8,128)(2,1)} %all-gather.2.cloned.1.call-done) | copy-start | bytes 4718596
  112.4 86.3 %collective-permute-start.1 = (f32[768,1280]{1,0:T(8,128)}, f32[768,1280]{1,0:T(8,128)}, u32[]{:S(2)}, u32[]{:S(2)}) collective-permute-start(f32[768,1280]{1,0:T(8,128)} %broadcast_select_fusion), channel_id=1, source_target_pairs={{0,16},{8,24},{16,32},{24,40},{32,48},{40,56},{48,64},{56,72},{64,... | collective-permute-start | bytes 11796488 | tf_op jit(solution)/shard_map/ppermute | solution.py:12
  112.4 18.4 %collective-permute-start.6 = (bf16[768,1024]{1,0:T(8,128)(2,1)S(1)}, bf16[768,1024]{1,0:T(8,128)(2,1)S(1)}, u32[]{:S(2)}, u32[]{:S(2)}) collective-permute-start(bf16[768,1024]{1,0:T(8,128)(2,1)S(1)} %copy-done), channel_id=1, source_target_pairs={{0,248},{8,0},{16,8},{24,16},{32,24},{40,32},{48,40},{56,48},{64,5... | collective-permute-start | bytes 4718600 | tf_op jit(solution)/shard_map/ppermute | solution.py:12
  131.0 72.2 %collective-permute-start.7 = (bf16[768,1024]{1,0:T(8,128)(2,1)S(1)}, bf16[768,1024]{1,0:T(8,128)(2,1)}, u32[]{:S(2)}, u32[]{:S(2)}) collective-permute-start(bf16[768,1024]{1,0:T(8,128)(2,1)S(1)} %broadcast_select_fusion.2), channel_id=1, source_target_pairs={{0,240},{8,248},{16,0},{24,8},{32,16},{40,24},{48,32},{56,40},{64,... | collective-permute-start | bytes 4718600 | tf_op jit(solution)/shard_map/ppermute | solution.py:12
  203.1 129.2 %collective-permute-start.2 = (f32[768,1280]{1,0:T(8,128)}, f32[768,1280]{1,0:T(8,128)}, u32[]{:S(2)}, u32[]{:S(2)}) collective-permute-start(f32[768,1280]{1,0:T(8,128)} %broadcast_select_fusion.1), channel_id=1, source_target_pairs={{0,32},{8,40},{16,48},{24,56},{32,64},{40,72},{48,80},{56,88},{64,... | collective-permute-start | bytes 11796488 | tf_op jit(solution)/shard_map/ppermute | solution.py:12
  203.3 124.1 %collective-permute-start.8 = (bf16[768,1024]{1,0:T(8,128)(2,1)S(1)}, bf16[768,1024]{1,0:T(8,128)(2,1)S(1)}, u32[]{:S(2)}, u32[]{:S(2)}) collective-permute-start(bf16[768,1024]{1,0:T(8,128)(2,1)S(1)} %broadcast_select_fusion.3), channel_id=1, source_target_pairs={{0,224},{8,232},{16,240},{24,248},{32,0},{40,8},{48,16},{56,24},{6... | collective-permute-start | bytes 4718600 | tf_op jit(solution)/shard_map/ppermute | solution.py:12
  209.0 1.3 collective-permute-start.3
  210.4 112.0 %collective-permute-start.4 = (s32[8,1,8]{2,0,1:T(8,128)S(1)}, s32[8,1,8]{2,0,1:T(8,128)S(1)}, u32[]{:S(2)}, u32[]{:S(2)}) collective-permute-start(s32[8,1,8]{2,0,1:T(8,128)S(1)} %broadcast_select_fusion.4), channel_id=1, source_target_pairs={{0,240},{8,248},{16,0},{24,8},{32,16},{40,24},{48,32},{56,40},{64,... | collective-permute-start | bytes 776 | tf_op jit(solution)/shard_map/ppermute | solution.py:12
  322.4 5.1 %collective-permute-start.5 = (s32[8,1,8]{2,0,1:T(8,128)S(1)}, s32[8,1,8]{2,0,1:T(8,128)S(1)}, u32[]{:S(2)}, u32[]{:S(2)}) collective-permute-start(s32[8,1,8]{2,0,1:T(8,128)S(1)} %broadcast_select_fusion.5), channel_id=1, source_target_pairs={{0,224},{8,232},{16,240},{24,248},{32,0},{40,8},{48,16},{56,24},{6... | collective-permute-start | bytes 776 | tf_op jit(solution)/shard_map/ppermute | solution.py:12
  327.6 1.9 copy-start.2
Sparse Core Ops, SparseCore 0:
  9.1 42.2 all-gather.1
  337.2 52.2 reduce-scatter.1
where the time goes:
time: 400 us; the launch traced here: 396 us
  waiting for transfers between devices  216 us (54%)
  starting transfers between devices  124 us (31%)
  blocking collectives  17.1 us (4%)
  other arithmetic  14.2 us (4%)
  between operations  13.5 us (3%)
  matrix products  9.54 us (2%)
    ppermute x9, waiting for transfers between devices, from_behind(): return lax.ppermute(value, axis, pairs)  135 us
    ppermute x9, starting transfers between devices, from_behind(): return lax.ppermute(value, axis, pairs)  124 us
    reduce_scatter x1, waiting for transfers between devices, shards(): lax.psum_scatter(carried + mirror, 'pair', scatter_dimension=0, tiled=True)  52.4 us
    all_gather x1, waiting for transfers between devices, shards(): lax.all_gather(l_tiles, 'pair', axis=0, tiled=True)  27.1 us
    all_gather x1, blocking collectives, shards(): lax.all_gather(nz_lists, 'pair', axis=0, tiled=True)  17.1 us
    select_n x2, other arithmetic, shards(): carried = jnp.where(chosen, arrived, carried)  8.93 us
  transfers between devices with their start and end apart: 11, of which 8 were waited for; matrix products, arithmetic and copies ran while one was open for 2% of the time, Pallas kernels for 0%

commit v1 on v0

v1 whole, which is shorter than its diff:
```python
import functools

import jax
import jax.numpy as jnp
from jax import lax
from jax.experimental import pallas as pl
from jax.experimental.pallas import tpu as pltpu
from jax.sharding import PartitionSpec as P

MESH = pl.DeviceIdType.MESH
B = 128
KB = 10
NZ = 8
P_DEV = 96
W = B * KB
NB = 8
NG = 32
MSG = NZ * P_DEV + 16
CB = 256
HALF = 4 * P_DEV
REL = (4, 3, -3, 2, -2, 1, -1, 0)
SLOT = {rel: slot for slot, rel in enumerate(REL)}
SLOT[-4] = SLOT[4]
QMAX = 32767.0


def encode(values):
    top = jnp.maximum(jnp.max(jnp.abs(values), axis=0, keepdims=True), 1e-30)
    coded = jnp.round(values * (QMAX / top)).astype(jnp.int32).astype(jnp.int16)
    return coded, top * (1.0 / QMAX)


def decode(coded, scale):
    return coded.astype(jnp.int32).astype(jnp.float32) * scale


def columns(j):
    return pl.ds(pl.multiple_of(j * CB, CB), CB)


def kernel(
    nz_ref, l_ref, v_ref, out_ref,
    own, far, dense_own, dense_far, v_dir, v_mir, mirror,
    d_out, d_out_sc, d_in, d_in_sc, r_out, r_out_sc, r_in, r_in_sc,
    v_sem, ag_s, ag_r, far_s, far_r, d_s, d_r, dsc_s, dsc_r, r_s, r_r, rsc_s, rsc_r,
):
    t = lax.axis_index("tile")
    z = lax.axis_index("pair")
    up = (t, lax.rem(z + 1, NB))
    down = (t, lax.rem(z + NB - 1, NB))
    ahead = (lax.rem(t + z, NG), z)
    behind = (lax.rem(t + NG - z, NG), z)
    shifted = z > 0

    loads = [
        pltpu.make_async_copy(v_ref.at[0, 0], v_dir, v_sem.at[0]),
        pltpu.make_async_copy(v_ref.at[0, 0], v_mir, v_sem.at[1]),
    ]
    for load in loads:
        load.start()

    barrier = pltpu.get_barrier_semaphore()
    for device in (up, down):
        pl.semaphore_signal(barrier, inc=1, device_id=device, device_id_type=MESH)

    @pl.when(shifted)
    def _():
        for device in (ahead, behind):
            pl.semaphore_signal(barrier, inc=1, device_id=device, device_id_type=MESH)

    me = SLOT[0]
    for e in range(NZ):
        own[me, e * P_DEV:(e + 1) * P_DEV, :] = l_ref[:, e * B:(e + 1) * B]
    entry = lax.broadcasted_iota(jnp.int32, (16, B), 0)
    listed = jnp.zeros((16, B), jnp.int32)
    for e in range(NZ):
        listed = jnp.where(entry == e, nz_ref[0, 0, e], listed)
    own[me, NZ * P_DEV:, :] = listed.astype(jnp.float32).astype(jnp.bfloat16)

    pl.semaphore_wait(barrier, 2 + 2 * jnp.minimum(z, 1))

    def remote(src, dst, send, recv, device):
        return pltpu.make_async_remote_copy(
            src_ref=src, dst_ref=dst, send_sem=send, recv_sem=recv,
            device_id=device, device_id_type=MESH,
        )

    def gather_copy(rel, step):
        src, dst = SLOT[rel], SLOT[rel - step]
        return remote(own.at[src], own.at[dst], ag_s.at[dst], ag_r.at[dst], up if step == 1 else down)

    def far_copy(slot):
        return remote(far_src(slot), far.at[slot], far_s.at[slot], far_r.at[slot], behind)

    def far_src(slot):
        return own.at[slot]

    def d_copies(slot):
        return (
            remote(d_out.at[slot], d_in.at[slot], d_s.at[slot], d_r.at[slot], ahead),
            remote(d_out_sc.at[slot], d_in_sc.at[slot], dsc_s.at[slot], dsc_r.at[slot], ahead),
        )

    def r_copies(rel, step):
        src, dst = SLOT[rel], SLOT[rel - step]
        lane = 0 if step == 1 else 1
        device = up if step == 1 else down
        return (
            remote(r_out.at[src], r_in.at[lane, dst], r_s.at[src], r_r.at[lane, dst], device),
            remote(r_out_sc.at[src], r_in_sc.at[lane, dst], rsc_s.at[src], rsc_r.at[lane, dst], device),
        )

    def expand(msg, slot, dense):
        lists = msg[slot, NZ * P_DEV:, :].astype(jnp.float32)
        for k in range(KB):
            total = None
            for e in range(max(0, k - KB + NZ), min(NZ - 1, k) + 1):
                hit = jnp.where(lists[e:e + 1, :] == float(k), 1.0, 0.0).astype(jnp.bfloat16)
                term = msg[slot, e * P_DEV:(e + 1) * P_DEV, :] * hit
                total = term if total is None else total + term
            dense[slot * P_DEV:(slot + 1) * P_DEV, k * B:(k + 1) * B] = total

    gather_sends = []

    def gather_start(rel, step):
        copy = gather_copy(rel, step)
        copy.start()
        gather_sends.append(copy)

    def far_start(slot):
        @pl.when(shifted)
        def _():
            far_copy(slot).start()

    gather_start(0, 1)
    gather_start(0, -1)
    far_start(me)
    for load in loads:
        load.wait()

    @pl.when(z == 0)
    def _():
        def mask(i, carry):
            rows = pl.ds(pl.multiple_of(i * B, B), B)
            row_ids = lax.broadcasted_iota(jnp.int32, (B, W), 0) + i * B
            col_ids = lax.broadcasted_iota(jnp.int32, (B, W), 1)
            block = v_dir[rows, :].astype(jnp.float32)
            v_dir[rows, :] = jnp.where(row_ids <= col_ids, block, 0.0).astype(jnp.bfloat16)
            v_mir[rows, :] = jnp.where(row_ids < col_ids, block, 0.0).astype(jnp.bfloat16)
            return carry

        lax.fori_loop(0, KB, mask, 0)

    expand(own, me, dense_own)

    for r in range(1, 5):
        gather_copy(-r + 1, 1).wait_recv()
        if r < 4:
            gather_start(-r, 1)
        far_start(SLOT[-r])
        if r < 4:
            gather_copy(r - 1, -1).wait_recv()
            if r < 3:
                gather_start(r, -1)
            far_start(SLOT[r])
        expand(own, SLOT[-r], dense_own)
        if r < 4:
            expand(own, SLOT[r], dense_own)

    def direct_half(first):
        def block(j, carry):
            part = jnp.dot(
                dense_own[first * P_DEV:first * P_DEV + HALF, :], v_dir[:, columns(j)],
                preferred_element_type=jnp.float32,
            )
            for i in range(4):
                coded, scale = encode(part[i * P_DEV:(i + 1) * P_DEV])
                d_out[first + i, :, columns(j)] = coded
                d_out_sc[first + i, :, columns(j)] = scale
            return carry

        lax.fori_loop(0, W // CB, block, 0)

        @pl.when(shifted)
        def _():
            for i in range(4):
                for copy in d_copies(first + i):
                    copy.start()

    def mirror_half(first):
        for slot in reversed(range(first, first + 4)):
            @pl.when(shifted)
            def _(slot=slot):
                far_copy(slot).wait_recv()
                expand(far, slot, dense_far)

        def block(j, carry):
            @pl.when(shifted)
            def _():
                mirror[first * P_DEV:first * P_DEV + HALF, columns(j)] = lax.dot_general(
                    dense_far[first * P_DEV:first * P_DEV + HALF, :], v_mir[columns(j), :],
                    (((1,), (1,)), ((), ())), preferred_element_type=jnp.float32,
                )

            @pl.when(z == 0)
            def _():
                mirror[first * P_DEV:first * P_DEV + HALF, columns(j)] = lax.dot_general(
                    dense_own[first * P_DEV:first * P_DEV + HALF, :], v_mir[columns(j), :],
                    (((1,), (1,)), ((), ())), preferred_element_type=jnp.float32,
                )
            return carry

        lax.fori_loop(0, W // CB, block, 0)

    direct_half(0)
    direct_half(4)
    mirror_half(4)
    mirror_half(0)

    def settle(slot, lanes, last):
        @pl.when(shifted)
        def _():
            for copy in d_copies(slot):
                copy.wait_recv()

        def block(j, carry):
            cols = columns(j)
            total = mirror[slot * P_DEV:(slot + 1) * P_DEV, cols]
            for lane in lanes:
                total = total + decode(r_in[lane, slot, :, cols], r_in_sc[lane, slot, :, cols])

            def finish(total):
                if last:
                    out_ref[:, cols] = total
                else:
                    coded, scale = encode(total)
                    r_out[slot, :, cols] = coded
                    r_out_sc[slot, :, cols] = scale

            @pl.when(shifted)
            def _():
                finish(total + decode(d_in[slot, :, cols], d_in_sc[slot, :, cols]))

            @pl.when(z == 0)
            def _():
                finish(total + decode(d_out[slot, :, cols], d_out_sc[slot, :, cols]))

            return carry

        lax.fori_loop(0, W // CB, block, 0)

    sum_sends = []
    for far_off in range(4, 0, -1):
        for step in (-1, 1):
            rel = far_off * step
            if rel == 4:
                continue
            slot = SLOT[rel]
            lanes = []
            if far_off < (4 if step == -1 else 3):
                for copy in r_copies(rel + step, step):
                    copy.wait_recv()
                lanes = [0 if step == 1 else 1]
            settle(slot, lanes, False)
            for copy in r_copies(rel, step):
                copy.start()
                sum_sends.append(copy)
    for step in (-1, 1):
        for copy in r_copies(step, step):
            copy.wait_recv()
    settle(me, [0, 1], True)

    for copy in gather_sends + sum_sends:
        copy.wait_send()

    @pl.when(shifted)
    def _():
        for slot in range(NB):
            far_copy(slot).wait_send()
            for copy in d_copies(slot):
                copy.wait_send()


def shards(l_tiles, nz_lists, v_slab):
    dma = pltpu.SemaphoreType.DMA
    return pl.pallas_call(
        kernel,
        out_shape=jax.ShapeDtypeStruct((P_DEV, W), jnp.float32),
        in_specs=[
            pl.BlockSpec(memory_space=pltpu.SMEM),
            pl.BlockSpec(memory_space=pltpu.VMEM),
            pl.BlockSpec(memory_space=pl.ANY),
        ],
        out_specs=pl.BlockSpec(memory_space=pltpu.VMEM),
        scratch_shapes=[
            pltpu.VMEM((NB, MSG, B), jnp.bfloat16),
            pltpu.VMEM((NB, MSG, B), jnp.bfloat16),
            pltpu.VMEM((NB * P_DEV, W), jnp.bfloat16),
            pltpu.VMEM((NB * P_DEV, W), jnp.bfloat16),
            pltpu.VMEM((W, W), jnp.bfloat16),
            pltpu.VMEM((W, W), jnp.bfloat16),
            pltpu.VMEM((NB * P_DEV, W), jnp.float32),
            pltpu.VMEM((NB, P_DEV, W), jnp.int16),
            pltpu.VMEM((NB, 1, W), jnp.float32),
            pltpu.VMEM((NB, P_DEV, W), jnp.int16),
            pltpu.VMEM((NB, 1, W), jnp.float32),
            pltpu.VMEM((NB, P_DEV, W), jnp.int16),
            pltpu.VMEM((NB, 1, W), jnp.float32),
            pltpu.VMEM((2, NB, P_DEV, W), jnp.int16),
            pltpu.VMEM((2, NB, 1, W), jnp.float32),
            dma((2,)),
            dma((NB,)), dma((NB,)),
            dma((NB,)), dma((NB,)),
            dma((NB,)), dma((NB,)), dma((NB,)), dma((NB,)),
            dma((NB,)), dma((2, NB)), dma((NB,)), dma((2, NB)),
        ],
        compiler_params=pltpu.CompilerParams(
            collective_id=0, has_side_effects=True, vmem_limit_bytes=48 << 20
        ),
    )(nz_lists, l_tiles, v_slab)


def solution(mesh):
    placed = (P("pair", "tile"), P("pair", "tile", None), P("tile", "pair", None, None))
    return jax.shard_map(
        shards, mesh=mesh, in_specs=placed, out_specs=P("pair", "tile"), check_vma=False
    )
```

time: 400 us -> 99.1 us (0.25)
  the two profiles are of different devices: /device:TPU:32 before, /device:TPU:61 now
where the time goes in v1:
time: 99.1 us; the launch traced here: 98.9 us
  Pallas kernels  94.6 us (95%)
  local copies, waits for them, and re-layouts  4.29 us (4%)
    pallas_call x1, Pallas kernels, shards(): pl.pallas_call(kernel, out_shape=jax.ShapeDtypeStruct((P_DEV, W), jnp.flo...  94.6 us
    unnamed x7, local copies, waits for them, and re-layouts  4.29 us

profile of v1, /device:TPU:61, one launch (start us, length us, event | category | flops | bytes accessed | tf_op | source)
XLA Modules:
  0.0 98.9 jit_solution(13165088841647577086)
XLA Ops:
  0.0 0.0 copy-start
  0.0 1.9 %copy-done = bf16[1,1,1280,1280]{3,2,1,0:T(8,128)(2,1)S(1)} copy-done((bf16[1,1,1280,1280]{3,2,1,0:T(8,128)(2,1)S(1)}, bf16[1,1,1280,1280]{3,2,1,0:T(8,128)(2,1)}, u32[]{:S(2)}) %copy-start) | copy-done | bytes 3276824
  1.9 0.0 copy-start.1
  1.9 0.9 copy-done.1
  2.9 0.0 copy-start.2
  2.9 0.7 copy-done.2
  3.5 94.6 %shard_map.37 = f32[96,1280]{1,0:T(8,128)S(1)} custom-call(s32[1,1,8]{2,1,0:T(1,128)S(1)} %copy-done.2, bf16[96,1024]{1,0:T(8,128)(2,1)S(1)} %copy-done.1, bf16[1,1,1280,1280]{3,2,1,0:T(8,128)(2,1)S(1)} %copy-done), custom_call_target="tpu_custom_call" | custom-call | tf_op jit(solution)/shard_map/pallas_call | solution.py:286
  98.2 0.8 copy.5
Async XLA Ops:
  0.0 1.9 %copy-start = (bf16[1,1,1280,1280]{3,2,1,0:T(8,128)(2,1)S(1)}, bf16[1,1,1280,1280]{3,2,1,0:T(8,128)(2,1)}, u32[]{:S(2)}) copy-start(bf16[1,1,1280,1280]{3,2,1,0:T(8,128)(2,1)} %v_ref.1) | copy-start | bytes 9830404
  1.9 0.9 copy-start.1
  2.9 0.7 copy-start.2

commit v2 on v1

--- a/solution.py
+++ b/solution.py
@@ -22,6 +22,19 @@
 SLOT = {rel: slot for slot, rel in enumerate(REL)}
 SLOT[-4] = SLOT[4]
 QMAX = 32767.0
+SHARED = (4, 5)
+LOW_TAKES = (0, -1, -2, -3)
+LOW_GETS = (1, 2, 3, 4)
+HIGH_TAKES = (0, 1, 2, 3)
+HIGH_GETS = (-1, -2, -3, 4)
+
+
+def near(rel):
+    return (rel + 3) % NB - 3
+
+
+def either(flags):
+    return functools.reduce(jnp.logical_or, flags)
 
 
 def encode(values):
@@ -40,9 +53,10 @@
 
 def kernel(
     nz_ref, l_ref, v_ref, out_ref,
-    own, far, dense_own, dense_far, v_dir, v_mir, mirror,
-    d_out, d_out_sc, d_in, d_in_sc, r_out, r_out_sc, r_in, r_in_sc,
-    v_sem, ag_s, ag_r, far_s, far_r, d_s, d_r, dsc_s, dsc_r, r_s, r_r, rsc_s, rsc_r,
+    lists, own, far, dense_own, dense_far, v_dir, v_mir, mirror,
+    d_out, d_out_sc, d_in, d_in_sc, r_out, r_out_sc, r_in, r_in_sc, p_in, p_in_sc,
+    l_sem, v_sem, ag_s, ag_r, far_s, far_r, d_s, d_r, dsc_s, dsc_r, r_s, r_r, rsc_s, rsc_r,
+    fwd_s, p_s, p_r, psc_s, psc_r,
 ):
     t = lax.axis_index("tile")
     z = lax.axis_index("pair")
@@ -52,6 +66,43 @@
     behind = (lax.rem(t + NG - z, NG), z)
     shifted = z > 0
 
+    core = lax.rem(t, 2)
+    core_behind = lax.rem(t + z, 2)
+    plane_low = either([z == k - 1 for k in SHARED])
+    plane_high = either([z == k for k in SHARED])
+    low = (core == 1) & plane_low
+    high = (core == 0) & plane_high
+    mate = (t + 1 - 2 * core, z + 2 * core - 1)
+    behind_low = (core_behind == 1) & plane_low
+    behind_high = (core_behind == 0) & plane_high
+
+    def behind_takes(rel):
+        flag = shifted
+        if rel in LOW_GETS:
+            flag = flag & jnp.logical_not(behind_low)
+        if rel in HIGH_GETS:
+            flag = flag & jnp.logical_not(behind_high)
+        return flag
+
+    def handed(rel):
+        flags = []
+        if rel in LOW_GETS:
+            flags.append(low)
+        if rel in HIGH_GETS:
+            flags.append(high)
+        return flags
+
+    me = SLOT[0]
+    list_load = pltpu.make_async_copy(nz_ref, lists, l_sem.at[NZ])
+    tile_loads = [
+        pltpu.make_async_copy(
+            l_ref.at[:, e * B:(e + 1) * B], own.at[me, e * P_DEV:(e + 1) * P_DEV, :], l_sem.at[e]
+        )
+        for e in range(NZ)
+    ]
+    list_load.start()
+    for load in tile_loads:
+        load.start()
     loads = [
         pltpu.make_async_copy(v_ref.at[0, 0], v_dir, v_sem.at[0]),
         pltpu.make_async_copy(v_ref.at[0, 0], v_mir, v_sem.at[1]),
@@ -68,16 +119,20 @@
         for device in (ahead, behind):
             pl.semaphore_signal(barrier, inc=1, device_id=device, device_id_type=MESH)
 
-    me = SLOT[0]
-    for e in range(NZ):
-        own[me, e * P_DEV:(e + 1) * P_DEV, :] = l_ref[:, e * B:(e + 1) * B]
+    @pl.when(low | high)
+    def _():
+        pl.semaphore_signal(barrier, inc=1, device_id=mate, device_id_type=MESH)
+
+    list_load.wait()
     entry = lax.broadcasted_iota(jnp.int32, (16, B), 0)
     listed = jnp.zeros((16, B), jnp.int32)
     for e in range(NZ):
-        listed = jnp.where(entry == e, nz_ref[0, 0, e], listed)
+        listed = jnp.where(entry == e, lists[0, 0, e], listed)
     own[me, NZ * P_DEV:, :] = listed.astype(jnp.float32).astype(jnp.bfloat16)
 
-    pl.semaphore_wait(barrier, 2 + 2 * jnp.minimum(z, 1))
+    pl.semaphore_wait(barrier, 2 + 2 * jnp.minimum(z, 1) + (low | high).astype(jnp.int32))
+    for load in tile_loads:
+        load.wait()
 
     def remote(src, dst, send, recv, device):
         return pltpu.make_async_remote_copy(
@@ -90,10 +145,18 @@
         return remote(own.at[src], own.at[dst], ag_s.at[dst], ag_r.at[dst], up if step == 1 else down)
 
     def far_copy(slot):
-        return remote(far_src(slot), far.at[slot], far_s.at[slot], far_r.at[slot], behind)
-
-    def far_src(slot):
-        return own.at[slot]
+        return remote(own.at[slot], far.at[slot], far_s.at[slot], far_r.at[slot], behind)
+
+    def hand_far(rel, step):
+        src, dst = SLOT[rel], SLOT[near(rel - step)]
+        return remote(far.at[src], far.at[dst], fwd_s.at[src], far_r.at[dst], mate)
+
+    def hand_part(rel, step):
+        src, dst = SLOT[rel], SLOT[near(rel - step)]
+        return (
+            remote(d_out.at[src], p_in.at[dst], p_s.at[src], p_r.at[dst], mate),
+            remote(d_out_sc.at[src], p_in_sc.at[dst], psc_s.at[src], psc_r.at[dst], mate),
+        )
 
     def d_copies(slot):
         return (
@@ -128,9 +191,17 @@
         gather_sends.append(copy)
 
     def far_start(slot):
-        @pl.when(shifted)
+        @pl.when(behind_takes(REL[slot]))
         def _():
             far_copy(slot).start()
+
+    def far_pass(rel):
+        for role, takes, step in ((low, LOW_TAKES, 1), (high, HIGH_TAKES, -1)):
+            if rel in takes:
+                @pl.when(role)
+                def _(step=step):
+                    far_copy(SLOT[rel]).wait_recv()
+                    hand_far(rel, step).start()
 
     gather_start(0, 1)
     gather_start(0, -1)
@@ -166,6 +237,58 @@
         expand(own, SLOT[-r], dense_own)
         if r < 4:
             expand(own, SLOT[r], dense_own)
+        far_pass(1 - r)
+        if r > 1:
+            far_pass(r - 1)
+
+    def d_send(slot):
+        rel = REL[slot]
+        paired = low | high
+
+        @pl.when(shifted & jnp.logical_not(paired))
+        def _():
+            for copy in d_copies(slot):
+                copy.start()
+
+        for role, gets, step in ((low, LOW_GETS, 1), (high, HIGH_GETS, -1)):
+            if rel in gets:
+                @pl.when(role)
+                def _(step=step):
+                    for copy in hand_part(rel, step):
+                        copy.start()
+
+    def d_merge(slot):
+        rel = REL[slot]
+        roles = []
+        if rel in LOW_TAKES:
+            roles.append(low)
+        if rel in HIGH_TAKES:
+            roles.append(high)
+
+        @pl.when(either(roles))
+        def _():
+            for copy in hand_part_in(slot):
+                copy.wait_recv()
+
+            def block(j, carry):
+                cols = columns(j)
+                coded, scale = encode(
+                    decode(d_out[slot, :, cols], d_out_sc[slot, :, cols])
+                    + decode(p_in[slot, :, cols], p_in_sc[slot, :, cols])
+                )
+                d_out[slot, :, cols] = coded
+                d_out_sc[slot, :, cols] = scale
+                return carry
+
+            lax.fori_loop(0, W // CB, block, 0)
+            for copy in d_copies(slot):
+                copy.start()
+
+    def hand_part_in(slot):
+        return (
+            remote(d_out.at[slot], p_in.at[slot], p_s.at[slot], p_r.at[slot], mate),
+            remote(d_out_sc.at[slot], p_in_sc.at[slot], psc_s.at[slot], psc_r.at[slot], mate),
+        )
 
     def direct_half(first):
         def block(j, carry):
@@ -181,17 +304,24 @@
 
         lax.fori_loop(0, W // CB, block, 0)
 
-        @pl.when(shifted)
-        def _():
-            for i in range(4):
-                for copy in d_copies(first + i):
-                    copy.start()
+        for slot in range(first, first + 4):
+            d_send(slot)
 
     def mirror_half(first):
         for slot in reversed(range(first, first + 4)):
+            rel = REL[slot]
+            fresh = shifted
+            if rel in LOW_TAKES:
+                fresh = fresh & jnp.logical_not(low)
+            if rel in HIGH_TAKES:
+                fresh = fresh & jnp.logical_not(high)
+
+            @pl.when(fresh)
+            def _(slot=slot):
+                far_copy(slot).wait_recv()
+
             @pl.when(shifted)
             def _(slot=slot):
-                far_copy(slot).wait_recv()
                 expand(far, slot, dense_far)
 
         def block(j, carry):
@@ -215,13 +345,29 @@
     direct_half(0)
     direct_half(4)
     mirror_half(4)
+    for slot in range(1, NB):
+        d_merge(slot)
     mirror_half(0)
 
     def settle(slot, lanes, last):
-        @pl.when(shifted)
+        def add_direct(part, part_sc):
+            def block(j, carry):
+                cols = columns(j)
+                rows = pl.ds(slot * P_DEV, P_DEV)
+                mirror[rows, cols] = mirror[rows, cols] + decode(part[slot, :, cols], part_sc[slot, :, cols])
+                return carry
+
+            lax.fori_loop(0, W // CB, block, 0)
+
+        @pl.when(behind_takes(REL[slot]))
         def _():
             for copy in d_copies(slot):
                 copy.wait_recv()
+            add_direct(d_in, d_in_sc)
+
+        @pl.when(z == 0)
+        def _():
+            add_direct(d_out, d_out_sc)
 
         def block(j, carry):
             cols = columns(j)
@@ -229,22 +375,12 @@
             for lane in lanes:
                 total = total + decode(r_in[lane, slot, :, cols], r_in_sc[lane, slot, :, cols])
 
-            def finish(total):
-                if last:
-                    out_ref[:, cols] = total
-                else:
-                    coded, scale = encode(total)
-                    r_out[slot, :, cols] = coded
-                    r_out_sc[slot, :, cols] = scale
-
-            @pl.when(shifted)
-            def _():
-                finish(total + decode(d_in[slot, :, cols], d_in_sc[slot, :, cols]))
-
-            @pl.when(z == 0)
-            def _():
-                finish(total + decode(d_out[slot, :, cols], d_out_sc[slot, :, cols]))
-
+            if last:
+                out_ref[:, cols] = total
+            else:
+                coded, scale = encode(total)
+                r_out[slot, :, cols] = coded
+                r_out_sc[slot, :, cols] = scale
             return carry
 
         lax.fori_loop(0, W // CB, block, 0)
@@ -273,12 +409,28 @@
     for copy in gather_sends + sum_sends:
         copy.wait_send()
 
-    @pl.when(shifted)
-    def _():
-        for slot in range(NB):
+    for slot, rel in enumerate(REL):
+        @pl.when(behind_takes(rel))
+        def _(slot=slot):
             far_copy(slot).wait_send()
+
+        direct_sent = shifted
+        for flag in handed(rel):
+            direct_sent = direct_sent & jnp.logical_not(flag)
+
+        @pl.when(direct_sent)
+        def _(slot=slot):
             for copy in d_copies(slot):
                 copy.wait_send()
+
+        for role, gets, takes, step in ((low, LOW_GETS, LOW_TAKES, 1), (high, HIGH_GETS, HIGH_TAKES, -1)):
+            @pl.when(role)
+            def _(rel=rel, gets=gets, step=step):
+                if rel in gets:
+                    for copy in hand_part(rel, step):
+                        copy.wait_send()
+                else:
+                    hand_far(rel, step).wait_send()
 
 
 def shards(l_tiles, nz_lists, v_slab):
@@ -287,12 +439,13 @@
         kernel,
         out_shape=jax.ShapeDtypeStruct((P_DEV, W), jnp.float32),
         in_specs=[
-            pl.BlockSpec(memory_space=pltpu.SMEM),
-            pl.BlockSpec(memory_space=pltpu.VMEM),
-            pl.BlockSpec(memory_space=pl.ANY),
+            pl.BlockSpec(memory_space=pltpu.HBM),
+            pl.BlockSpec(memory_space=pltpu.HBM),
+            pl.BlockSpec(memory_space=pltpu.HBM),
         ],
         out_specs=pl.BlockSpec(memory_space=pltpu.VMEM),
         scratch_shapes=[
+            pltpu.SMEM((1, 1, NZ), jnp.int32),
             pltpu.VMEM((NB, MSG, B), jnp.bfloat16),
             pltpu.VMEM((NB, MSG, B), jnp.bfloat16),
             pltpu.VMEM((NB * P_DEV, W), jnp.bfloat16),
@@ -308,14 +461,18 @@
             pltpu.VMEM((NB, 1, W), jnp.float32),
             pltpu.VMEM((2, NB, P_DEV, W), jnp.int16),
             pltpu.VMEM((2, NB, 1, W), jnp.float32),
+            pltpu.VMEM((NB, P_DEV, W), jnp.int16),
+            pltpu.VMEM((NB, 1, W), jnp.float32),
+            dma((NZ + 1,)),
             dma((2,)),
             dma((NB,)), dma((NB,)),
             dma((NB,)), dma((NB,)),
             dma((NB,)), dma((NB,)), dma((NB,)), dma((NB,)),
             dma((NB,)), dma((2, NB)), dma((NB,)), dma((2, NB)),
+            dma((NB,)), dma((NB,)), dma((NB,)), dma((NB,)), dma((NB,)),
         ],
         compiler_params=pltpu.CompilerParams(
-            collective_id=0, has_side_effects=True, vmem_limit_bytes=48 << 20
+            collective_id=0, has_side_effects=True, vmem_limit_bytes=63 << 20
         ),
     )(nz_lists, l_tiles, v_slab)
 

time: 99.1 us -> 87 us (0.88)
  the two profiles are of different devices: /device:TPU:61 before, /device:TPU:32 now
where the time goes in v2:
time: 87 us; the launch traced here: 85.4 us
  Pallas kernels  83.6 us (96%)
  local copies, waits for them, and re-layouts  1.84 us (2%)
    pallas_call x1, Pallas kernels, shards(): pl.pallas_call(kernel, out_shape=jax.ShapeDtypeStruct((P_DEV, W), jnp.flo...  83.6 us
    unnamed x1, local copies, waits for them, and re-layouts  1.84 us

profile of v2, /device:TPU:32, one launch (start us, length us, event | category | flops | bytes accessed | tf_op | source)
XLA Modules:
  0.0 85.4 jit_solution(13976568392631493415)
XLA Ops:
  0.0 83.6 %shard_map.37 = f32[96,1280]{1,0:T(8,128)} custom-call(s32[1,1,8]{2,1,0:T(1,128)} %nz_ref.1, bf16[96,1024]{1,0:T(8,128)(2,1)} %l_ref.1, bf16[1,1,1280,1280]{3,2,1,0:T(8,128)(2,1)} %v_ref.1), custom_call_target="tpu_custom_call" | custom-call | tf_op jit(solution)/shard_map/pallas_call | solution.py:438
  83.6 1.8 %copy.5 = f32[96,1280]{1,0:T(8,128)} copy(f32[96,1280]{1,0:T(8,128)} %shard_map.37) | data formatting | bytes 983040

commit v3 on v2

--- a/solution.py
+++ b/solution.py
@@ -17,20 +17,30 @@
 NG = 32
 MSG = NZ * P_DEV + 16
 CB = 256
-HALF = 4 * P_DEV
-REL = (4, 3, -3, 2, -2, 1, -1, 0)
+ROW_PIECES = ((0, 208), (208, 192), (400, 192), (592, 192))
+ROWS_UP = 2
+COL_PIECES = 2
+PW = W // COL_PIECES
+REL = (4, -3, 3, 2, -2, 1, -1, 0)
 SLOT = {rel: slot for slot, rel in enumerate(REL)}
 SLOT[-4] = SLOT[4]
 QMAX = 32767.0
-SHARED = (4, 5)
+SHARED = (2, 3, 4, 5, 6, 7)
 LOW_TAKES = (0, -1, -2, -3)
 LOW_GETS = (1, 2, 3, 4)
 HIGH_TAKES = (0, 1, 2, 3)
 HIGH_GETS = (-1, -2, -3, 4)
+MERGED = (2, 3, 4, 5, 6, 7)
+LOW_MERGES = (0, -1, -2, -3)
+LOW_LENDS = (1, 2, 3, 4)
 
 
 def near(rel):
     return (rel + 3) % NB - 3
+
+
+HIGH_MERGES = tuple(near(rel - 1) for rel in LOW_LENDS)
+HIGH_LENDS = tuple(near(rel - 1) for rel in LOW_MERGES)
 
 
 def either(flags):
@@ -73,6 +83,10 @@
     low = (core == 1) & plane_low
     high = (core == 0) & plane_high
     mate = (t + 1 - 2 * core, z + 2 * core - 1)
+    low_d = (core == 1) & either([z == k - 1 for k in MERGED])
+    high_d = (core == 0) & either([z == k for k in MERGED])
+    behind_low_d = (core_behind == 1) & either([z == k - 1 for k in MERGED])
+    behind_high_d = (core_behind == 0) & either([z == k for k in MERGED])
     behind_low = (core_behind == 1) & plane_low
     behind_high = (core_behind == 0) & plane_high
 
@@ -84,13 +98,29 @@
             flag = flag & jnp.logical_not(behind_high)
         return flag
 
-    def handed(rel):
-        flags = []
-        if rel in LOW_GETS:
-            flags.append(low)
-        if rel in HIGH_GETS:
-            flags.append(high)
-        return flags
+    def behind_sends(rel):
+        flag = shifted
+        if rel in LOW_LENDS:
+            flag = flag & jnp.logical_not(behind_low_d)
+        if rel in HIGH_LENDS:
+            flag = flag & jnp.logical_not(behind_high_d)
+        return flag
+
+    def lent(rel):
+        flag = z < 0
+        if rel in LOW_LENDS:
+            flag = flag | low_d
+        if rel in HIGH_LENDS:
+            flag = flag | high_d
+        return flag
+
+    def merges(rel):
+        flag = z < 0
+        if rel in LOW_MERGES:
+            flag = flag | low_d
+        if rel in HIGH_MERGES:
+            flag = flag | high_d
+        return flag
 
     me = SLOT[0]
     list_load = pltpu.make_async_copy(nz_ref, lists, l_sem.at[NZ])
@@ -103,12 +133,8 @@
     list_load.start()
     for load in tile_loads:
         load.start()
-    loads = [
-        pltpu.make_async_copy(v_ref.at[0, 0], v_dir, v_sem.at[0]),
-        pltpu.make_async_copy(v_ref.at[0, 0], v_mir, v_sem.at[1]),
-    ]
-    for load in loads:
-        load.start()
+    v_load = pltpu.make_async_copy(v_ref.at[0, 0], v_dir, v_sem.at[0])
+    v_load.start()
 
     barrier = pltpu.get_barrier_semaphore()
     for device in (up, down):
@@ -140,9 +166,13 @@
             device_id=device, device_id_type=MESH,
         )
 
-    def gather_copy(rel, step):
+    def gather_copy(rel, step, piece):
         src, dst = SLOT[rel], SLOT[rel - step]
-        return remote(own.at[src], own.at[dst], ag_s.at[dst], ag_r.at[dst], up if step == 1 else down)
+        rows = pl.ds(*ROW_PIECES[piece])
+        return remote(
+            own.at[src, rows], own.at[dst, rows], ag_s.at[dst, piece], ag_r.at[dst, piece],
+            up if step == 1 else down,
+        )
 
     def far_copy(slot):
         return remote(own.at[slot], far.at[slot], far_s.at[slot], far_r.at[slot], behind)
@@ -164,13 +194,20 @@
             remote(d_out_sc.at[slot], d_in_sc.at[slot], dsc_s.at[slot], dsc_r.at[slot], ahead),
         )
 
-    def r_copies(rel, step):
+    def r_copies(rel, step, piece):
         src, dst = SLOT[rel], SLOT[rel - step]
         lane = 0 if step == 1 else 1
         device = up if step == 1 else down
+        cols = pl.ds(piece * PW, PW)
         return (
-            remote(r_out.at[src], r_in.at[lane, dst], r_s.at[src], r_r.at[lane, dst], device),
-            remote(r_out_sc.at[src], r_in_sc.at[lane, dst], rsc_s.at[src], rsc_r.at[lane, dst], device),
+            remote(
+                r_out.at[src, :, cols], r_in.at[lane, dst, :, cols],
+                r_s.at[src, piece], r_r.at[lane, dst, piece], device,
+            ),
+            remote(
+                r_out_sc.at[src, :, cols], r_in_sc.at[lane, dst, :, cols],
+                rsc_s.at[src, piece], rsc_r.at[lane, dst, piece], device,
+            ),
         )
 
     def expand(msg, slot, dense):
@@ -185,8 +222,8 @@
 
     gather_sends = []
 
-    def gather_start(rel, step):
-        copy = gather_copy(rel, step)
+    def gather_start(rel, step, piece):
+        copy = gather_copy(rel, step, piece)
         copy.start()
         gather_sends.append(copy)
 
@@ -203,69 +240,54 @@
                     far_copy(SLOT[rel]).wait_recv()
                     hand_far(rel, step).start()
 
-    gather_start(0, 1)
-    gather_start(0, -1)
+    for piece in range(len(ROW_PIECES)):
+        gather_start(0, 1, piece)
+        gather_start(0, -1, piece)
     far_start(me)
-    for load in loads:
-        load.wait()
-
-    @pl.when(z == 0)
-    def _():
-        def mask(i, carry):
-            rows = pl.ds(pl.multiple_of(i * B, B), B)
+    v_load.wait()
+
+    def turn(i, carry):
+        rows = pl.ds(pl.multiple_of(i * B, B), B)
+
+        @pl.when(shifted)
+        def _():
+            v_mir[:, rows] = v_dir[rows, :].T
+
+        @pl.when(z == 0)
+        def _():
             row_ids = lax.broadcasted_iota(jnp.int32, (B, W), 0) + i * B
             col_ids = lax.broadcasted_iota(jnp.int32, (B, W), 1)
             block = v_dir[rows, :].astype(jnp.float32)
             v_dir[rows, :] = jnp.where(row_ids <= col_ids, block, 0.0).astype(jnp.bfloat16)
-            v_mir[rows, :] = jnp.where(row_ids < col_ids, block, 0.0).astype(jnp.bfloat16)
-            return carry
-
-        lax.fori_loop(0, KB, mask, 0)
-
+            v_mir[:, rows] = jnp.where(row_ids < col_ids, block, 0.0).astype(jnp.bfloat16).T
+
+        return carry
+
+    lax.fori_loop(0, KB, turn, 0)
     expand(own, me, dense_own)
 
-    for r in range(1, 5):
-        gather_copy(-r + 1, 1).wait_recv()
-        if r < 4:
-            gather_start(-r, 1)
-        far_start(SLOT[-r])
-        if r < 4:
-            gather_copy(r - 1, -1).wait_recv()
-            if r < 3:
-                gather_start(r, -1)
-            far_start(SLOT[r])
-        expand(own, SLOT[-r], dense_own)
-        if r < 4:
-            expand(own, SLOT[r], dense_own)
-        far_pass(1 - r)
-        if r > 1:
-            far_pass(r - 1)
-
-    def d_send(slot):
-        rel = REL[slot]
-        paired = low | high
-
-        @pl.when(shifted & jnp.logical_not(paired))
+    def d_send(rel):
+        slot = SLOT[rel]
+
+        @pl.when(shifted & jnp.logical_not(lent(rel)) & jnp.logical_not(merges(rel)))
         def _():
             for copy in d_copies(slot):
                 copy.start()
 
-        for role, gets, step in ((low, LOW_GETS, 1), (high, HIGH_GETS, -1)):
-            if rel in gets:
+    def d_lend(rel):
+        for role, lends, step in ((low_d, LOW_LENDS, 1), (high_d, HIGH_LENDS, -1)):
+            if rel in lends:
                 @pl.when(role)
                 def _(step=step):
                     for copy in hand_part(rel, step):
                         copy.start()
 
-    def d_merge(slot):
-        rel = REL[slot]
-        roles = []
-        if rel in LOW_TAKES:
-            roles.append(low)
-        if rel in HIGH_TAKES:
-            roles.append(high)
-
-        @pl.when(either(roles))
+    def d_merge(rel):
+        slot = SLOT[rel]
+        if rel not in LOW_MERGES + HIGH_MERGES:
+            return
+
+        @pl.when(merges(rel))
         def _():
             for copy in hand_part_in(slot):
                 copy.wait_recv()
@@ -290,13 +312,15 @@
             remote(d_out_sc.at[slot], p_in_sc.at[slot], psc_s.at[slot], psc_r.at[slot], mate),
         )
 
-    def direct_half(first):
+    def direct(first, last):
+        count = last - first + 1
+
         def block(j, carry):
             part = jnp.dot(
-                dense_own[first * P_DEV:first * P_DEV + HALF, :], v_dir[:, columns(j)],
+                dense_own[first * P_DEV:(last + 1) * P_DEV, :], v_dir[:, columns(j)],
                 preferred_element_type=jnp.float32,
             )
-            for i in range(4):
+            for i in range(count):
                 coded, scale = encode(part[i * P_DEV:(i + 1) * P_DEV])
                 d_out[first + i, :, columns(j)] = coded
                 d_out_sc[first + i, :, columns(j)] = scale
@@ -304,53 +328,94 @@
 
         lax.fori_loop(0, W // CB, block, 0)
 
-        for slot in range(first, first + 4):
-            d_send(slot)
-
-    def mirror_half(first):
-        for slot in reversed(range(first, first + 4)):
-            rel = REL[slot]
-            fresh = shifted
-            if rel in LOW_TAKES:
-                fresh = fresh & jnp.logical_not(low)
-            if rel in HIGH_TAKES:
-                fresh = fresh & jnp.logical_not(high)
-
-            @pl.when(fresh)
-            def _(slot=slot):
-                far_copy(slot).wait_recv()
-
-            @pl.when(shifted)
-            def _(slot=slot):
-                expand(far, slot, dense_far)
+    def far_wait(slot):
+        rel = REL[slot]
+        fresh = shifted
+        if rel in LOW_TAKES:
+            fresh = fresh & jnp.logical_not(low)
+        if rel in HIGH_TAKES:
+            fresh = fresh & jnp.logical_not(high)
+
+        @pl.when(fresh)
+        def _():
+            far_copy(slot).wait_recv()
+
+        @pl.when(shifted)
+        def _():
+            expand(far, slot, dense_far)
+
+    def mirrored(first, last):
+        for slot in range(last, first - 1, -1):
+            far_wait(slot)
+        rows = slice(first * P_DEV, (last + 1) * P_DEV)
 
         def block(j, carry):
-            @pl.when(shifted)
-            def _():
-                mirror[first * P_DEV:first * P_DEV + HALF, columns(j)] = lax.dot_general(
-                    dense_far[first * P_DEV:first * P_DEV + HALF, :], v_mir[columns(j), :],
-                    (((1,), (1,)), ((), ())), preferred_element_type=jnp.float32,
-                )
-
-            @pl.when(z == 0)
-            def _():
-                mirror[first * P_DEV:first * P_DEV + HALF, columns(j)] = lax.dot_general(
-                    dense_own[first * P_DEV:first * P_DEV + HALF, :], v_mir[columns(j), :],
-                    (((1,), (1,)), ((), ())), preferred_element_type=jnp.float32,
-                )
+            for flag, dense in ((shifted, dense_far), (z == 0, dense_own)):
+                @pl.when(flag)
+                def _(dense=dense):
+                    mirror[rows, columns(j)] = jnp.dot(
+                        dense[rows, :], v_mir[:, columns(j)], preferred_element_type=jnp.float32
+                    )
             return carry
 
         lax.fori_loop(0, W // CB, block, 0)
 
-    direct_half(0)
-    direct_half(4)
-    mirror_half(4)
-    for slot in range(1, NB):
-        d_merge(slot)
-    mirror_half(0)
-
-    def settle(slot, lanes, last):
-        def add_direct(part, part_sc):
+    def gathered(r):
+        for piece in range(len(ROW_PIECES)):
+            if r < 4 or piece < ROWS_UP:
+                gather_copy(-r + 1, 1, piece).wait_recv()
+            if r < 3 or (r == 3 and piece < ROWS_UP):
+                gather_start(-r, 1, piece)
+            if r < 4 or piece >= ROWS_UP:
+                gather_copy(r - 1, -1, piece).wait_recv()
+            if r < 3 or (r == 3 and piece >= ROWS_UP):
+                gather_start(r, -1, piece)
+
+    direct(7, 7)
+    gathered(1)
+    far_start(SLOT[-1])
+    far_start(SLOT[1])
+    expand(own, SLOT[-1], dense_own)
+    expand(own, SLOT[1], dense_own)
+    direct(5, 6)
+    d_send(1)
+    d_send(-1)
+    far_pass(0)
+    gathered(2)
+    far_start(SLOT[-2])
+    expand(own, SLOT[-2], dense_own)
+    expand(own, SLOT[2], dense_own)
+    direct(3, 4)
+    d_send(2)
+    far_pass(-1)
+    far_pass(1)
+    gathered(3)
+    far_start(SLOT[-3])
+    expand(own, SLOT[-3], dense_own)
+    expand(own, SLOT[3], dense_own)
+    far_pass(-2)
+    gathered(4)
+    far_start(SLOT[4])
+    far_start(SLOT[3])
+    far_start(SLOT[2])
+    expand(own, SLOT[4], dense_own)
+    direct(0, 2)
+    d_send(4)
+    d_lend(4)
+    d_send(-3)
+    d_lend(-3)
+    d_send(3)
+    d_lend(3)
+    d_lend(2)
+    d_lend(-2)
+    d_lend(1)
+    d_lend(-1)
+    far_pass(-3)
+    far_pass(3)
+    far_pass(2)
+
+    def add_direct(slot):
+        def add(part, part_sc):
             def block(j, carry):
                 cols = columns(j)
                 rows = pl.ds(slot * P_DEV, P_DEV)
@@ -359,22 +424,22 @@
 
             lax.fori_loop(0, W // CB, block, 0)
 
-        @pl.when(behind_takes(REL[slot]))
+        @pl.when(behind_sends(REL[slot]))
         def _():
             for copy in d_copies(slot):
                 copy.wait_recv()
-            add_direct(d_in, d_in_sc)
+            add(d_in, d_in_sc)
 
         @pl.when(z == 0)
         def _():
-            add_direct(d_out, d_out_sc)
-
+            add(d_out, d_out_sc)
+
+    def settle(slot, piece, lanes, last):
         def block(j, carry):
-            cols = columns(j)
+            cols = pl.ds(pl.multiple_of(piece * PW + j * B, B), B)
             total = mirror[slot * P_DEV:(slot + 1) * P_DEV, cols]
             for lane in lanes:
                 total = total + decode(r_in[lane, slot, :, cols], r_in_sc[lane, slot, :, cols])
-
             if last:
                 out_ref[:, cols] = total
             else:
@@ -383,28 +448,51 @@
                 r_out_sc[slot, :, cols] = scale
             return carry
 
-        lax.fori_loop(0, W // CB, block, 0)
+        lax.fori_loop(0, PW // B, block, 0)
 
     sum_sends = []
-    for far_off in range(4, 0, -1):
-        for step in (-1, 1):
+
+    def relay(far_off):
+        for slot in sorted({SLOT[far_off], SLOT[-far_off]}):
+            add_direct(slot)
+        for step, piece in ((1, 0), (-1, 1), (-1, 0), (1, 1)):
+            begins = (step, piece) in ((1, 0), (-1, 1))
+            if far_off == 4 and begins:
+                continue
             rel = far_off * step
-            if rel == 4:
-                continue
-            slot = SLOT[rel]
             lanes = []
-            if far_off < (4 if step == -1 else 3):
-                for copy in r_copies(rel + step, step):
+            if far_off < 3 or (far_off == 3 and not begins):
+                for copy in r_copies(rel + step, step, piece):
                     copy.wait_recv()
                 lanes = [0 if step == 1 else 1]
-            settle(slot, lanes, False)
-            for copy in r_copies(rel, step):
+            settle(SLOT[rel], piece, lanes, False)
+            for copy in r_copies(rel, step, piece):
                 copy.start()
                 sum_sends.append(copy)
-    for step in (-1, 1):
-        for copy in r_copies(step, step):
-            copy.wait_recv()
-    settle(me, [0, 1], True)
+
+    mirrored(4, 7)
+    d_merge(-3)
+    d_merge(3)
+    mirrored(0, 0)
+    relay(4)
+    d_send(-2)
+    d_merge(-2)
+    d_merge(2)
+    mirrored(1, 2)
+    relay(3)
+    d_send(0)
+    d_merge(-1)
+    d_merge(1)
+    d_merge(0)
+    mirrored(3, 3)
+    relay(2)
+    relay(1)
+    add_direct(me)
+    for piece in range(COL_PIECES):
+        for step in (-1, 1):
+            for copy in r_copies(step, step, piece):
+                copy.wait_recv()
+        settle(me, piece, [0, 1], True)
 
     for copy in gather_sends + sum_sends:
         copy.wait_send()
@@ -414,23 +502,23 @@
         def _(slot=slot):
             far_copy(slot).wait_send()
 
-        direct_sent = shifted
-        for flag in handed(rel):
-            direct_sent = direct_sent & jnp.logical_not(flag)
-
-        @pl.when(direct_sent)
+        @pl.when(shifted & jnp.logical_not(lent(rel)))
         def _(slot=slot):
             for copy in d_copies(slot):
                 copy.wait_send()
 
-        for role, gets, takes, step in ((low, LOW_GETS, LOW_TAKES, 1), (high, HIGH_GETS, HIGH_TAKES, -1)):
-            @pl.when(role)
-            def _(rel=rel, gets=gets, step=step):
-                if rel in gets:
+        for role, takes, step in ((low, LOW_TAKES, 1), (high, HIGH_TAKES, -1)):
+            if rel in takes:
+                @pl.when(role)
+                def _(rel=rel, step=step):
+                    hand_far(rel, step).wait_send()
+
+        for role, lends, step in ((low_d, LOW_LENDS, 1), (high_d, HIGH_LENDS, -1)):
+            if rel in lends:
+                @pl.when(role)
+                def _(rel=rel, step=step):
                     for copy in hand_part(rel, step):
                         copy.wait_send()
-                else:
-                    hand_far(rel, step).wait_send()
 
 
 def shards(l_tiles, nz_lists, v_slab):
@@ -464,11 +552,11 @@
             pltpu.VMEM((NB, P_DEV, W), jnp.int16),
             pltpu.VMEM((NB, 1, W), jnp.float32),
             dma((NZ + 1,)),
-            dma((2,)),
-            dma((NB,)), dma((NB,)),
+            dma((1,)),
+            dma((NB, len(ROW_PIECES))), dma((NB, len(ROW_PIECES))),
             dma((NB,)), dma((NB,)),
             dma((NB,)), dma((NB,)), dma((NB,)), dma((NB,)),
-            dma((NB,)), dma((2, NB)), dma((NB,)), dma((2, NB)),
+            dma((NB, 2)), dma((2, NB, 2)), dma((NB, 2)), dma((2, NB, 2)),
             dma((NB,)), dma((NB,)), dma((NB,)), dma((NB,)), dma((NB,)),
         ],
         compiler_params=pltpu.CompilerParams(

time: 87 us -> 75.8 us (0.87); the launches traced: 85.4 us -> 75.4 us
  Pallas kernels: 83.6 us -> 73.5 us
    pallas_call x1, Pallas kernels: 83.6 us -> 73.5 us  [shards(): pl.pallas_call(kernel, out_shape=jax.ShapeDtypeStruct((P_DEV, W), jnp.flo...]
where the time goes in v3:
time: 75.8 us; the launch traced here: 75.4 us
  Pallas kernels  73.5 us (97%)
  local copies, waits for them, and re-layouts  1.84 us (2%)
    pallas_call x1, Pallas kernels, shards(): pl.pallas_call(kernel, out_shape=jax.ShapeDtypeStruct((P_DEV, W), jnp.flo...  73.5 us
    unnamed x1, local copies, waits for them, and re-layouts  1.84 us

profile of v3, /device:TPU:32, one launch (start us, length us, event | category | flops | bytes accessed | tf_op | source)
XLA Modules:
  0.0 75.4 jit_solution(18129581713446435450)
XLA Ops:
  0.0 73.5 %shard_map.37 = f32[96,1280]{1,0:T(8,128)} custom-call(s32[1,1,8]{2,1,0:T(1,128)} %nz_ref.1, bf16[96,1024]{1,0:T(8,128)(2,1)} %l_ref.1, bf16[1,1,1280,1280]{3,2,1,0:T(8,128)(2,1)} %v_ref.1), custom_call_target="tpu_custom_call" | custom-call | tf_op jit(solution)/shard_map/pallas_call | solution.py:526
  73.6 1.8 %copy.5 = f32[96,1280]{1,0:T(8,128)} copy(f32[96,1280]{1,0:T(8,128)} %shard_map.37) | data formatting | bytes 983040

commit v4 on v3

--- a/solution.py
+++ b/solution.py
@@ -31,8 +31,8 @@
 HIGH_TAKES = (0, 1, 2, 3)
 HIGH_GETS = (-1, -2, -3, 4)
 MERGED = (2, 3, 4, 5, 6, 7)
-LOW_MERGES = (0, -1, -2, -3)
-LOW_LENDS = (1, 2, 3, 4)
+LOW_MERGES = (0, -1, -2)
+LOW_LENDS = (1, 2, 3)
 
 
 def near(rel):
@@ -372,6 +372,7 @@
                 gather_start(r, -1, piece)
 
     direct(7, 7)
+    d_send(0)
     gathered(1)
     far_start(SLOT[-1])
     far_start(SLOT[1])
@@ -383,36 +384,39 @@
     far_pass(0)
     gathered(2)
     far_start(SLOT[-2])
+    far_start(SLOT[2])
     expand(own, SLOT[-2], dense_own)
     expand(own, SLOT[2], dense_own)
     direct(3, 4)
     d_send(2)
+    d_send(-2)
     far_pass(-1)
     far_pass(1)
     gathered(3)
     far_start(SLOT[-3])
+    far_start(SLOT[3])
     expand(own, SLOT[-3], dense_own)
     expand(own, SLOT[3], dense_own)
+    direct(1, 2)
+    d_send(-3)
+    d_send(3)
     far_pass(-2)
+    far_pass(2)
     gathered(4)
     far_start(SLOT[4])
-    far_start(SLOT[3])
-    far_start(SLOT[2])
     expand(own, SLOT[4], dense_own)
-    direct(0, 2)
+    direct(0, 0)
     d_send(4)
     d_lend(4)
-    d_send(-3)
+    mirrored(4, 7)
+    far_pass(-3)
+    far_pass(3)
+    d_lend(3)
     d_lend(-3)
-    d_send(3)
-    d_lend(3)
     d_lend(2)
     d_lend(-2)
     d_lend(1)
     d_lend(-1)
-    far_pass(-3)
-    far_pass(3)
-    far_pass(2)
 
     def add_direct(slot):
         def add(part, part_sc):
@@ -453,13 +457,15 @@
     sum_sends = []
 
     def relay(far_off):
-        for slot in sorted({SLOT[far_off], SLOT[-far_off]}):
-            add_direct(slot)
+        added = set()
         for step, piece in ((1, 0), (-1, 1), (-1, 0), (1, 1)):
             begins = (step, piece) in ((1, 0), (-1, 1))
             if far_off == 4 and begins:
                 continue
             rel = far_off * step
+            if SLOT[rel] not in added:
+                added.add(SLOT[rel])
+                add_direct(SLOT[rel])
             lanes = []
             if far_off < 3 or (far_off == 3 and not begins):
                 for copy in r_copies(rel + step, step, piece):
@@ -470,19 +476,14 @@
                 copy.start()
                 sum_sends.append(copy)
 
-    mirrored(4, 7)
-    d_merge(-3)
-    d_merge(3)
+    d_merge(-2)
+    d_merge(2)
     mirrored(0, 0)
     relay(4)
-    d_send(-2)
-    d_merge(-2)
-    d_merge(2)
+    d_merge(-1)
+    d_merge(1)
     mirrored(1, 2)
     relay(3)
-    d_send(0)
-    d_merge(-1)
-    d_merge(1)
     d_merge(0)
     mirrored(3, 3)
     relay(2)

time: 75.8 us -> 71.4 us (0.942)
  Pallas kernels: 73.5 us -> 69.4 us
    pallas_call x1, Pallas kernels: 73.5 us -> 69.4 us  [shards(): pl.pallas_call(kernel, out_shape=jax.ShapeDtypeStruct((P_DEV, W), jnp.flo...]
where the time goes in v4:
time: 71.4 us; the launch traced here: 71.2 us
  Pallas kernels  69.4 us (97%)
  local copies, waits for them, and re-layouts  1.84 us (3%)
    pallas_call x1, Pallas kernels, shards(): pl.pallas_call(kernel, out_shape=jax.ShapeDtypeStruct((P_DEV, W), jnp.flo...  69.4 us
    unnamed x1, local copies, waits for them, and re-layouts  1.84 us

profile of v4, /device:TPU:32, one launch (start us, length us, event | category | flops | bytes accessed | tf_op | source)
XLA Modules:
  0.0 71.2 jit_solution(6719189409957596893)
XLA Ops:
  0.0 69.4 %shard_map.37 = f32[96,1280]{1,0:T(8,128)} custom-call(s32[1,1,8]{2,1,0:T(1,128)} %nz_ref.1, bf16[96,1024]{1,0:T(8,128)(2,1)} %l_ref.1, bf16[1,1,1280,1280]{3,2,1,0:T(8,128)(2,1)} %v_ref.1), custom_call_target="tpu_custom_call" | custom-call | tf_op jit(solution)/shard_map/pallas_call | solution.py:527
  69.4 1.8 %copy.5 = f32[96,1280]{1,0:T(8,128)} copy(f32[96,1280]{1,0:T(8,128)} %shard_map.37) | data formatting | bytes 983040

commit v5 on v4

--- a/solution.py
+++ b/solution.py
@@ -476,10 +476,10 @@
                 copy.start()
                 sum_sends.append(copy)
 
+    mirrored(0, 0)
+    relay(4)
     d_merge(-2)
     d_merge(2)
-    mirrored(0, 0)
-    relay(4)
     d_merge(-1)
     d_merge(1)
     mirrored(1, 2)

time: 71.4 us -> 71.2 us (level)
  no operation moved by 1% of the time
where the time goes in v5:
time: 71.2 us; the launch traced here: 71.1 us
  Pallas kernels  69.2 us (97%)
  local copies, waits for them, and re-layouts  1.84 us (3%)
    pallas_call x1, Pallas kernels, shards(): pl.pallas_call(kernel, out_shape=jax.ShapeDtypeStruct((P_DEV, W), jnp.flo...  69.2 us
    unnamed x1, local copies, waits for them, and re-layouts  1.84 us

profile of v5, /device:TPU:32, one launch (start us, length us, event | category | flops | bytes accessed | tf_op | source)
XLA Modules:
  0.0 71.1 jit_solution(7188105559470034459)
XLA Ops:
  0.0 69.2 %shard_map.37 = f32[96,1280]{1,0:T(8,128)} custom-call(s32[1,1,8]{2,1,0:T(1,128)} %nz_ref.1, bf16[96,1024]{1,0:T(8,128)(2,1)} %l_ref.1, bf16[1,1,1280,1280]{3,2,1,0:T(8,128)(2,1)} %v_ref.1), custom_call_target="tpu_custom_call" | custom-call | tf_op jit(solution)/shard_map/pallas_call | solution.py:527
  69.2 1.8 %copy.5 = f32[96,1280]{1,0:T(8,128)} copy(f32[96,1280]{1,0:T(8,128)} %shard_map.37) | data formatting | bytes 983040
